TPU v7x, 32 devices: a whole 2x2x4 slice. The times are simulated.
32 devices in a mesh: groups: 2 (over y), expert: 16 (over z, x, core).
Axes of the slice: x: 2, y: 2, z: 4, core: 2. Of those that a mesh axis runs over, the one named last changes fastest.
Arguments:
- routes: int32 [4096, 8], P(('groups', 'expert')), parts along dimension 0, may hold values from 0 to 15, all different within a row; in each aligned block of 128 rows (0 to 127, 128 to 255, ...) at most 128 rows name the same one
- acts: bfloat16 [4096, 2048], P(('groups', 'expert')), parts along dimension 0, may hold values from -36 to 36
- grads: bfloat16 [4096, 8, 768], P(('groups', 'expert')), parts along dimension 0, may hold values from -36 to 36
- weights: bfloat16 [32, 2048, 768], P(('groups', 'expert')), parts along dimension 0, may hold values from -6 to 6
- cluster: int32 [32], P('groups'), parts along dimension 0, may hold values from 0 to 7, as said below
Outputs:
- merged: float32 [16, 2048, 768], P('groups', 'expert'), parts along dimension 0
There are 2 independent parts, one for each index of `groups`. A program takes and returns all parts, laid end to end along the dimension named above; each array names one. Nothing has to cross between parts.
Inputs may be any that keep to these rules, and one draw needn't show every extreme that they name: `routes`: in the rows of one device no expert is named by more than 128 pairs; every expert is named by some pair; a token names 8 different experts. `cluster`: every merged expert has exactly two members.
All inputs are finite; a program needn't handle non-finite values.
Results may differ from a plain program's by a relative error of at most 0.00056.
Values may be sent and summed in bfloat16 or wider, within the bound.
A program may use at most 128 MiB of HBM per device.

v0:
```python
import jax
import jax.numpy as jnp
from jax import lax
from jax.sharding import PartitionSpec as P

PRIOR_WEIGHT = 1.0


def on_device(routes, acts, grads, weights, cluster):
    experts = lax.axis_size("expert")
    tok_rows, fanout = routes.shape
    model_cols = acts.shape[1]
    hidden = grads.shape[2]
    pair_count = tok_rows * fanout
    slot_count = 2 * pair_count // experts
    slab_rows = model_cols // experts
    expert_ids = jnp.arange(experts, dtype=jnp.int32)
    moved_w = lax.all_to_all(
        weights.reshape(experts, slab_rows, hidden),
        "expert",
        split_axis=0,
        concat_axis=0,
        tiled=True,
    )
    flat_ids = routes.reshape(pair_count)
    onehot = (flat_ids[:, None] == expert_ids[None, :]).astype(jnp.int32)
    running = jnp.cumsum(onehot, axis=0)
    position = jnp.sum(onehot * running, axis=1) - 1
    target = flat_ids * slot_count + position
    sq_act = jnp.square(acts.astype(jnp.float32)).astype(jnp.bfloat16)
    sq_grad = jnp.square(grads.astype(jnp.float32)).astype(jnp.bfloat16).reshape(pair_count, hidden)
    pair_act = jnp.repeat(sq_act, fanout, axis=0)
    send_act = jnp.zeros((experts * slot_count, model_cols), jnp.bfloat16).at[target].set(pair_act)
    send_act = send_act.reshape(experts, slot_count, model_cols)
    send_grad = jnp.zeros((experts * slot_count, hidden), jnp.bfloat16).at[target].set(sq_grad)
    send_grad = send_grad.reshape(experts, slot_count, hidden)
    totals = lax.psum(jnp.sum(onehot, axis=0), "expert")
    own_index = lax.axis_index("expert")
    own_count = jnp.sum(jnp.where(expert_ids == own_index, totals, 0)).astype(jnp.float32)
    got_act, got_grad = (
        lax.all_to_all(send_act, "expert", split_axis=0, concat_axis=0, tiled=True),
        lax.all_to_all(send_grad, "expert", split_axis=0, concat_axis=0, tiled=True),
    )
    fisher_sum = lax.dot_general(
        got_act.reshape(experts * slot_count, model_cols),
        got_grad.reshape(experts * slot_count, hidden),
        (((0,), (0,)), ((), ())),
        preferred_element_type=jnp.float32,
    )
    precision = fisher_sum / own_count + PRIOR_WEIGHT
    member = (cluster[None, :] == jnp.arange(experts // 2, dtype=jnp.int32)[:, None]).astype(
        jnp.float32
    )
    moved_p = lax.all_to_all(
        precision.reshape(experts, slab_rows, hidden),
        "expert",
        split_axis=0,
        concat_axis=0,
        tiled=True,
    )
    scaled = moved_p * moved_w.astype(jnp.float32)
    numerator = jnp.einsum("ce,erf->crf", member, scaled, precision=lax.Precision.HIGHEST)
    denominator = jnp.einsum("ce,erf->crf", member, moved_p, precision=lax.Precision.HIGHEST)
    return numerator / denominator


def solution(mesh):
    return jax.shard_map(
        on_device,
        mesh=mesh,
        in_specs=(
            P(("groups", "expert"), None),
            P(("groups", "expert"), None),
            P(("groups", "expert"), None, None),
            P(("groups", "expert"), None, None),
            P("groups"),
        ),
        out_specs=P("groups", "expert", None),
        check_vma=False,
    )
```

profile of v0, /device:TPU:0, one launch (start us, length us, event | category | flops | bytes accessed | tf_op | source)
XLA Modules:
  0.0 525.4 jit_solution(18175032873814915357)
XLA Ops:
  0.0 0.8 copy.20
  0.8 0.1 eq.51
  0.9 0.1 eq.47
  1.0 0.7 broadcast_multiply_fusion
  1.7 4.5 reduce-window.6
  6.2 0.1 slice.8
  6.3 0.1 copy.22
  6.4 0.1 copy.23
  6.5 0.1 broadcast_add_fusion
  6.6 0.1 convert_reduce_fusion
  6.7 0.1 copy.19
  6.8 0.1 mul.24
  7.0 7.9 %scatter_custom_fusion.1 = bf16[2048,768]{1,0:T(8,128)(2,1)} fusion(s32[1024]{0:T(1024)S(1)} %bitcast.42, bf16[128,8,768]{2,1,0:T(8,128)(2,1)} %param.7, bf16[]{:T(256)} %constant.7.clone.1), kind=kCustom, calls=%fused_computation.16 | custom fusion | flops 2359296 | bytes 4718594 | tf_op jit(solution)/shard_map/scatter | solution.py:35
  14.9 7.4 %all-to-all-start.1 = ((bf16[16,128,768]{2,1,0:T(8,128)(2,1)}), bf16[16,128,768]{2,1,0:T(8,128)(2,1)S(1)}, u32[]{:S(2)}, u32[]{:S(2)}) async-start(bf16[16,128,768]{2,1,0:T(8,128)(2,1)} %bitcast.8), calls=%async_computation.1 | async-start | bytes 6291456 | tf_op jit(solution)/shard_map/all_to_all | solution.py:42
  22.2 2.0 multiply_convert_fusion.1
  24.2 11.7 %scatter_custom_fusion = bf16[2048,2048]{1,0:T(8,128)(2,1)} fusion(s32[1024]{0:T(1024)S(1)} %bitcast.43, bf16[]{:T(256)} %constant.7.clone.1, bf16[128,2048]{1,0:T(8,128)(2,1)} %multiply_convert_fusion.1), kind=kCustom, calls=%fused_computation.9 | custom fusion | bytes 8912898 | tf_op jit(solution)/shard_map/scatter | solution.py:33
  35.9 12.3 %copy.24 = bf16[16,128,2048]{1,2,0:T(8,128)(2,1)} copy(bf16[16,128,2048]{2,1,0:T(8,128)(2,1)} %bitcast.36) | data formatting | bytes 16777216 | tf_op jit(solution)/shard_map/reshape | solution.py:34
  48.2 33.4 %all-to-all-done.1 = bf16[16,128,768]{2,1,0:T(8,128)(2,1)S(1)} async-done(((bf16[16,128,768]{2,1,0:T(8,128)(2,1)}), bf16[16,128,768]{2,1,0:T(8,128)(2,1)S(1)}, u32[]{:S(2)}, u32[]{:S(2)}) %all-to-all-start.1) | async-done | bytes 3145760 | tf_op jit(solution)/shard_map/all_to_all | solution.py:42
  81.6 0.0 copy-start
  81.6 197.7 %all_to_all.20 = bf16[16,128,2048]{1,2,0:T(8,128)(2,1)} all-to-all(bf16[16,128,2048]{1,2,0:T(8,128)(2,1)} %copy.24), channel_id=1, replica_groups=mesh['groups'=2,'expert'=16] {'expert'}, dimensions={0} | all-to-all | bytes 16777216 | tf_op jit(solution)/shard_map/all_to_all | solution.py:41
  279.3 0.0 copy-done
  279.3 5.7 %all-to-all-start.3 = ((bf16[16,128,768]{2,1,0:T(8,128)(2,1)}), bf16[16,128,768]{2,1,0:T(8,128)(2,1)S(1)}, u32[]{:S(2)}, u32[]{:S(2)}) async-start(bf16[16,128,768]{2,1,0:T(8,128)(2,1)} %bitcast.38), calls=%async_computation.3 | async-start | bytes 6291456 | tf_op jit(solution)/shard_map/all_to_all | solution.py:18
  285.0 71.8 %psum.7 = s32[16]{0:T(128)S(1)} all-reduce(s32[16]{0:T(128)S(1)} %get-tuple-element.5), channel_id=1, replica_groups=mesh['groups'=2,'expert'=16] {'expert'}, use_global_device_ids=true, to_apply=%region_6.7 | all-reduce | flops 16 | bytes 128 | tf_op jit(solution)/shard_map/psum | solution.py:37
  356.7 0.6 fusion.24
  357.9 11.4 %fusion = f32[2048,768]{1,0:T(8,128)} fusion(bf16[16,128,2048]{1,2,0:T(8,128)(2,1)} %all_to_all.20, bf16[16,128,768]{2,1,0:T(8,128)(2,1)} %copy-done, f32[]{:T(128)S(6)} %convert_element_type.32), kind=kOutput, calls=%fused_computation.3 | convolution fusion | flops 6445596672 | bytes 17825796 | tf_op jit(solution)/shard_map/dot_general | solution.py:44
  369.3 0.0 all-to-all-done.3
  369.3 140.9 %all_to_all.21 = f32[16,128,768]{2,1,0:T(8,128)S(1)} all-to-all(f32[16,128,768]{2,1,0:T(8,128)} %bitcast.37), channel_id=1, replica_groups=mesh['groups'=2,'expert'=16] {'expert'}, dimensions={0} | all-to-all | bytes 12582912 | tf_op jit(solution)/shard_map/all_to_all | solution.py:54
  510.2 0.0 copy-start.1
  510.2 0.7 convert_multiply_fusion
  510.9 0.0 copy-done.1
  510.9 5.8 %fusion.1 = f32[8,128,768]{2,0,1:T(8,128)S(1)} fusion(f32[16,128,768]{2,1,0:T(8,128)S(1)} %all_to_all.21, s32[16]{0:T(128)S(1)} %copy-done.1), kind=kOutput, calls=%fused_computation.4 | convolution fusion | flops 150995072 | bytes 9437248 | tf_op jit(solution)/shard_map/ce,erf->crf/dot_general | solution.py:63
  516.7 6.0 %fusion.9 = f32[8,128,768]{2,0,1:T(8,128)S(1)} fusion(f32[8,128,768]{2,0,1:T(8,128)S(1)} %fusion.1, f32[16,128,768]{2,1,0:T(8,128)S(1)} %convert_multiply_fusion, s32[16]{0:T(128)S(1)} %copy-done.1), kind=kOutput, calls=%fused_computation.14 | convolution fusion | flops 151781504 | bytes 12582976 | tf_op jit(solution)/shard_map/ce,erf->crf/dot_general | solution.py:62
  522.8 2.6 copy.27
  (5 shorter events, 0.1 us)
Async XLA Ops:
  14.9 66.7 %all-to-all-start.1 = ((bf16[16,128,768]{2,1,0:T(8,128)(2,1)}), bf16[16,128,768]{2,1,0:T(8,128)(2,1)S(1)}, u32[]{:S(2)}, u32[]{:S(2)}) async-start(bf16[16,128,768]{2,1,0:T(8,128)(2,1)} %bitcast.8), calls=%async_computation.1 | async-start | bytes 6291456 | tf_op jit(solution)/shard_map/all_to_all | solution.py:42
  81.6 197.7 %copy-start = (bf16[16,128,768]{2,1,0:T(8,128)(2,1)}, bf16[16,128,768]{2,1,0:T(8,128)(2,1)S(1)}, u32[]{:S(2)}) copy-start(bf16[16,128,768]{2,1,0:T(8,128)(2,1)S(1)} %all-to-all-done.1) | copy-start | bytes 9437188
  279.3 90.0 %all-to-all-start.3 = ((bf16[16,128,768]{2,1,0:T(8,128)(2,1)}), bf16[16,128,768]{2,1,0:T(8,128)(2,1)S(1)}, u32[]{:S(2)}, u32[]{:S(2)}) async-start(bf16[16,128,768]{2,1,0:T(8,128)(2,1)} %bitcast.38), calls=%async_computation.3 | async-start | bytes 6291456 | tf_op jit(solution)/shard_map/all_to_all | solution.py:18
  510.2 0.7 copy-start.1
where the time goes:
time: 527 us; the launch traced here: 525 us
  blocking collectives  410 us (78%)
  waiting for transfers between devices  33.4 us (6%)
  local copies, waits for them, and re-layouts  28 us (5%)
  matrix products  23.2 us (4%)
  other arithmetic  16.7 us (3%)
  starting transfers between devices  13 us (2%)
    all_to_all x1, blocking collectives, on_device(): lax.all_to_all(send_act, 'expert', split_axis=0, concat_axis=0, tiled=True)  198 us
    all_to_all x1, blocking collectives, on_device(): lax.all_to_all(precision.reshape(experts, slab_rows, hidden), 'expert', s...  141 us
    psum x1, blocking collectives, on_device(): totals = lax.psum(jnp.sum(onehot, axis=0), 'expert')  71.8 us
    all_to_all x1, waiting for transfers between devices, on_device(): lax.all_to_all(send_grad, 'expert', split_axis=0, concat_axis=0, tiled=True)  33.4 us
    reshape x1, local copies, waits for them, and re-layouts, on_device(): send_act = send_act.reshape(experts, slot_count, model_cols)  12.3 us
    scatter x1, local copies, waits for them, and re-layouts, on_device(): jnp.zeros((experts * slot_count, model_cols), jnp.bfloat16).at[target]  11.7 us
    dot_general x1, matrix products, on_device(): lax.dot_general(got_act.reshape(experts * slot_count, model_cols), got_gr...  11.4 us
  transfers between devices with their start and end apart: 2, of which 1 were waited for; matrix products, arithmetic and copies ran while one was open for 7% of the time, Pallas kernels for 0%

commit v1 on v0

--- a/solution.py
+++ b/solution.py
@@ -1,12 +1,20 @@
+import functools
+
 import jax
 import jax.numpy as jnp
 from jax import lax
+from jax.experimental import pallas as pl
+from jax.experimental.pallas import tpu as pltpu
 from jax.sharding import PartitionSpec as P
 
 PRIOR_WEIGHT = 1.0
-
-
-def on_device(routes, acts, grads, weights, cluster):
+CHUNKS = 2
+X_LAG = 2
+VMEM_BYTES = 56 * 2**20
+GATHER_BYTES = 32 * 2**20
+
+
+def routed(routes, acts, grads, weights, cluster):
     experts = lax.axis_size("expert")
     tok_rows, fanout = routes.shape
     model_cols = acts.shape[1]
@@ -64,6 +72,312 @@
     return numerator / denominator
 
 
+def merge_kernel(
+    n,
+    routes_ref,
+    acts_ref,
+    grads_ref,
+    weights_ref,
+    cluster_ref,
+    out_ref,
+    rt_v,
+    act_v,
+    g_v,
+    w_v,
+    acc,
+    lhs,
+    gsq,
+    rep,
+    cnt,
+    inv,
+    rt_send,
+    rt_recv,
+    act_send,
+    act_recv,
+    w_send,
+    w_recv,
+    g_send,
+    g_recv,
+):
+    nz = n // 4
+    slab = act_v.shape[2]
+    rows = g_v.shape[2]
+    hidden = g_v.shape[3]
+    fanout = rows * CHUNKS // act_v.shape[1]
+    me = lax.axis_index("expert")
+    core = lax.rem(me, 2)
+    x = lax.rem(me // 2, 2)
+    z = me // 4
+    x_peer = (z * 2 + (1 - x)) * 2 + core
+    sibling = (z * 2 + x) * 2 + (1 - core)
+
+    def far(i):
+        return lax.rem(me + i, n)
+
+    barrier = pltpu.get_barrier_semaphore()
+
+    @pl.loop(1, n)
+    def _(i):
+        pl.semaphore_signal(
+            barrier, inc=1, device_id={"expert": far(i)}, device_id_type=pl.DeviceIdType.MESH
+        )
+
+    pl.semaphore_wait(barrier, n - 1)
+
+    def remote(src, dst, send, recv, peer):
+        return pltpu.make_async_remote_copy(
+            src_ref=src,
+            dst_ref=dst,
+            send_sem=send,
+            recv_sem=recv,
+            device_id={"expert": peer},
+            device_id_type=pl.DeviceIdType.MESH,
+        )
+
+    def columns(owner):
+        return acts_ref.at[:, pl.ds(pl.multiple_of(owner * slab, slab), slab)]
+
+    def weight_rows(owner):
+        return weights_ref.at[pl.ds(pl.multiple_of(owner * slab, slab), slab)]
+
+    def rt_copy(peer):
+        return remote(routes_ref, rt_v.at[me], rt_send.at[peer], rt_recv.at[me], peer)
+
+    def act_copy(peer):
+        return remote(columns(peer), act_v.at[me], act_send.at[peer], act_recv.at[me], peer)
+
+    def w_copy(peer):
+        return remote(weight_rows(peer), w_v.at[me], w_send.at[peer], w_recv.at[me], peer)
+
+    def own_rows(j):
+        return grads_ref.at[pl.ds(pl.multiple_of(j * rows, rows), rows)]
+
+    def g_copy(b, j, kind, peer):
+        return remote(
+            g_v.at[b, j], g_v.at[b, j], g_send.at[kind, b, j], g_recv.at[b, j], peer
+        )
+
+    def g_own_copy(j, kind, peer):
+        return remote(own_rows(j), g_v.at[me, j], g_send.at[kind, me, j], g_recv.at[me, j], peer)
+
+    def arrived(dst, sem):
+        pltpu.make_async_copy(dst, dst, sem).wait()
+
+    pltpu.make_async_copy(routes_ref, rt_v.at[me], rt_recv.at[me]).start()
+    pltpu.make_async_copy(columns(me), act_v.at[me], act_recv.at[me]).start()
+
+    @pl.loop(1, n)
+    def _(i):
+        rt_copy(far(i)).start()
+        act_copy(far(i)).start()
+
+    @pl.loop(0, CHUNKS)
+    def _(j):
+        @pl.when(z > 0)
+        def _():
+            g_own_copy(j, 0, me - 4).start()
+
+        @pl.when(z < nz - 1)
+        def _():
+            g_own_copy(j, 1, me + 4).start()
+
+        g_own_copy(j, 2, x_peer).start()
+        g_own_copy(j, 3, sibling).start()
+        pltpu.make_async_copy(own_rows(j), g_v.at[me, j], g_recv.at[me, j]).start()
+
+    pltpu.make_async_copy(weight_rows(me), w_v.at[me], w_recv.at[me]).start()
+
+    acc[...] = jnp.zeros_like(acc)
+    cnt[...] = jnp.zeros_like(cnt)
+    token = lax.broadcasted_iota(jnp.int32, (act_v.shape[1], rows), 0)
+    pair = lax.broadcasted_iota(jnp.int32, (act_v.shape[1], rows), 1)
+    for j in range(CHUNKS):
+        rep[j] = jnp.where(token == (pair + j * rows) // fanout, 1.0, 0.0).astype(jnp.bfloat16)
+
+    def add_block(b, j):
+        grad = g_v[b, j].astype(jnp.float32)
+        gsq[...] = (grad * grad).astype(jnp.bfloat16)
+        act = act_v[b].astype(jnp.float32)
+        sq_act = (act * act).astype(jnp.bfloat16)
+        wide = lax.dot_general(
+            sq_act, rep[j], (((0,), (0,)), ((), ())), preferred_element_type=jnp.float32
+        ).astype(jnp.bfloat16)
+        named = rt_v[b, j]
+        ids = lax.broadcasted_iota(jnp.int32, (n, rows), 0)
+        mask = jnp.where(ids == named, 1.0, 0.0)
+        cnt[...] += mask
+        for e in range(n):
+            keep = jnp.broadcast_to(mask[e : e + 1].astype(jnp.bfloat16), (slab, rows))
+            lhs[e * slab : (e + 1) * slab, :] = wide * keep
+        step = 256 if hidden % 256 == 0 else hidden
+        for k in range(0, hidden, step):
+            acc[:, :, k : k + step] += jnp.dot(
+                lhs[...], gsq[:, k : k + step], preferred_element_type=jnp.float32
+            ).reshape(n, slab, step)
+
+    turns = (nz + X_LAG) * CHUNKS
+    burst = -(-(n - 1) // (turns // 2))
+
+    @pl.loop(0, turns)
+    def _(turn):
+        r = turn // CHUNKS
+        j = lax.rem(turn, CHUNKS)
+        for k in range(burst):
+            i = turn * burst + k + 1
+
+            @pl.when(i < n)
+            def _(i=i):
+                w_copy(far(i)).start()
+
+        @pl.loop(0, 8)
+        def _(q):
+            other_core = q // 4
+            other_x = lax.rem(q // 2, 2)
+            up = lax.rem(q, 2)
+            dist = r - X_LAG * other_x
+            z0 = z + (2 * up - 1) * dist
+            b = (z0 * 2 + lax.rem(x + other_x, 2)) * 2 + lax.rem(core + other_core, 2)
+            inside = (dist >= 0) & (dist < nz) & (z0 >= 0) & (z0 < nz)
+
+            @pl.when(inside & ((dist > 0) | (up == 0)))
+            def _():
+                arrived(g_v.at[b, j], g_recv.at[b, j])
+
+                @pl.when((other_core == 0) & (b != me))
+                def _():
+                    @pl.when(other_x == 0)
+                    def _():
+                        @pl.when((up == 1) & (z > 0))
+                        def _():
+                            g_copy(b, j, 0, me - 4).start()
+
+                        @pl.when((up == 0) & (z < nz - 1))
+                        def _():
+                            g_copy(b, j, 1, me + 4).start()
+
+                        g_copy(b, j, 2, x_peer).start()
+
+                    g_copy(b, j, 3, sibling).start()
+
+                @pl.when(j == 0)
+                def _():
+                    arrived(rt_v.at[b], rt_recv.at[b])
+                    arrived(act_v.at[b], act_recv.at[b])
+
+                add_block(b, j)
+
+    share = 1.0 / jnp.sum(cnt[...], axis=1, keepdims=True)
+    for e in range(n):
+        inv[e] = jnp.broadcast_to(share[e : e + 1], inv.shape[1:])
+
+    @pl.loop(0, n)
+    def _(e):
+        arrived(w_v.at[e], w_recv.at[e])
+
+    @pl.loop(0, n // 2)
+    def _(c):
+        first = jnp.int32(n - 1)
+        second = jnp.int32(0)
+        for e in range(n):
+            hit = cluster_ref[e] == c
+            first = jnp.where(hit, jnp.minimum(first, e), first)
+            second = jnp.where(hit, jnp.maximum(second, e), second)
+        p_one = acc[first] * inv[first][:1, :1] + PRIOR_WEIGHT
+        p_two = acc[second] * inv[second][:1, :1] + PRIOR_WEIGHT
+        w_one = w_v[first].astype(jnp.float32)
+        w_two = w_v[second].astype(jnp.float32)
+        out_ref[c] = (p_one * w_one + p_two * w_two) / (p_one + p_two)
+
+    @pl.loop(1, n)
+    def _(i):
+        rt_copy(far(i)).wait_send()
+        act_copy(far(i)).wait_send()
+        w_copy(far(i)).wait_send()
+
+    @pl.loop(0, n * CHUNKS)
+    def _(s):
+        b = s // CHUNKS
+        j = lax.rem(s, CHUNKS)
+        z0 = b // 4
+        same_core = lax.rem(b, 2) == core
+        same_column = same_core & (lax.rem(b // 2, 2) == x)
+
+        @pl.when(same_column & (z0 >= z) & (z > 0))
+        def _():
+            g_copy(b, j, 0, me - 4).wait_send()
+
+        @pl.when(same_column & (z0 <= z) & (z < nz - 1))
+        def _():
+            g_copy(b, j, 1, me + 4).wait_send()
+
+        @pl.when(same_column)
+        def _():
+            g_copy(b, j, 2, x_peer).wait_send()
+
+        @pl.when(same_core)
+        def _():
+            g_copy(b, j, 3, sibling).wait_send()
+
+
+def gathered(routes, acts, grads, weights, cluster):
+    n = lax.axis_size("expert")
+    tok_rows, fanout = routes.shape
+    hidden = grads.shape[2]
+    slab = acts.shape[1] // n
+    pairs = tok_rows * fanout
+    rows = pairs // CHUNKS
+    anywhere = pl.BlockSpec(memory_space=pl.ANY)
+    dma = pltpu.SemaphoreType.DMA
+    bf16 = jnp.bfloat16
+    return pl.pallas_call(
+        functools.partial(merge_kernel, n),
+        out_shape=jax.ShapeDtypeStruct((n // 2, slab, hidden), jnp.float32),
+        in_specs=[anywhere] * 4 + [pl.BlockSpec(memory_space=pltpu.SMEM)],
+        out_specs=pl.BlockSpec(memory_space=pltpu.VMEM),
+        scratch_shapes=[
+            pltpu.VMEM((n, CHUNKS, 1, rows), jnp.int32),
+            pltpu.VMEM((n, tok_rows, slab), bf16),
+            pltpu.VMEM((n, CHUNKS, rows, hidden), bf16),
+            pltpu.VMEM((n, slab, hidden), bf16),
+            pltpu.VMEM((n, slab, hidden), jnp.float32),
+            pltpu.VMEM((n * slab, rows), bf16),
+            pltpu.VMEM((rows, hidden), bf16),
+            pltpu.VMEM((CHUNKS, tok_rows, rows), bf16),
+            pltpu.VMEM((n, rows), jnp.float32),
+            pltpu.VMEM((n, 8, 128), jnp.float32),
+            dma((n,)),
+            dma((n,)),
+            dma((n,)),
+            dma((n,)),
+            dma((n,)),
+            dma((n,)),
+            dma((4, n, CHUNKS)),
+            dma((n, CHUNKS)),
+        ],
+        compiler_params=pltpu.CompilerParams(
+            collective_id=0, has_side_effects=True, vmem_limit_bytes=VMEM_BYTES
+        ),
+        cost_estimate=pl.CostEstimate(
+            flops=2 * n * pairs * n * slab * hidden,
+            bytes_accessed=2 * n * pairs * hidden,
+            transcendentals=0,
+        ),
+    )(
+        routes.reshape(CHUNKS, 1, rows),
+        acts,
+        grads.reshape(pairs, hidden),
+        weights.reshape(n * slab, hidden),
+        cluster,
+    )
+
+
+def on_device(routes, acts, grads, weights, cluster):
+    n = lax.axis_size("expert")
+    if n % 4 or 2 * n * grads.size > GATHER_BYTES:
+        return routed(routes, acts, grads, weights, cluster)
+    return gathered(routes, acts, grads, weights, cluster)
+
+
 def solution(mesh):
     return jax.shard_map(
         on_device,

time: 527 us -> 211 us (0.40)
  blocking collectives: 410 us -> 0 us
  Pallas kernels: 0 us -> 203 us
  waiting for transfers between devices: 33.4 us -> 0 us
  matrix products: 23.2 us -> 0 us
  local copies, waits for them, and re-layouts: 28 us -> 5.27 us
  other arithmetic: 16.7 us -> 0 us
  starting transfers between devices: 13 us -> 0 us
    all_to_all x2 -> x0, blocking collectives: 339 us -> none  [the longest x1 198 us: on_device(): lax.all_to_all(send_act, 'expert', split_axis=0, concat_axis=0, tiled=True)]
    pallas_call x0 -> x1, Pallas kernels: none -> 203 us  [gathered(): pl.pallas_call(functools.partial(merge_kernel, n), out_shape=jax.ShapeDty...]
    psum x1 -> x0, blocking collectives: 71.8 us -> none  [on_device(): totals = lax.psum(jnp.sum(onehot, axis=0), 'expert')]
    all_to_all x2 -> x0, waiting for transfers between devices: 33.4 us -> none  [the longest x1 33.4 us: on_device(): lax.all_to_all(send_grad, 'expert', split_axis=0, concat_axis=0, tiled=True)]
    dot_general x3 -> x0, matrix products: 23.2 us -> none  [the longest x1 11.4 us: on_device(): lax.dot_general(got_act.reshape(experts * slot_count, model_cols), got_gr...]
    all_to_all x2 -> x0, starting transfers between devices: 13 us -> none  [the longest x1 7.36 us: on_device(): lax.all_to_all(send_grad, 'expert', split_axis=0, concat_axis=0, tiled=True)]
    scatter x1 -> x0, local copies, waits for them, and re-layouts: 11.7 us -> none  [on_device(): jnp.zeros((experts * slot_count, model_cols), jnp.bfloat16).at[target]]
    reshape x1, local copies, waits for them, and re-layouts: 12.3 us -> 0.69 us  [gathered(): routes.reshape(CHUNKS, 1, rows)]
  transfers between devices with their start and end apart: 2 -> 0, of which waited for: 1 -> 0; matrix products, arithmetic and copies ran while one was open for 7% -> 0% of each run, Pallas kernels for 0% -> 0%
where the time goes in v1:
time: 211 us; the launch traced here: 209 us
  Pallas kernels  203 us (96%)
  local copies, waits for them, and re-layouts  5.27 us (2%)
    pallas_call x1, Pallas kernels, gathered(): pl.pallas_call(functools.partial(merge_kernel, n), out_shape=jax.ShapeDty...  203 us
    unnamed x2, local copies, waits for them, and re-layouts  4.57 us

profile of v1, /device:TPU:0, one launch (start us, length us, event | category | flops | bytes accessed | tf_op | source)
XLA Modules:
  0.0 208.6 jit_solution(17898182831953818565)
XLA Ops:
  0.0 0.8 copy.7
  0.8 0.7 reshape.12.routes_ref
  1.5 203.4 %shard_map.55 = f32[8,128,768]{2,1,0:T(8,128)} custom-call(s32[2,1,512]{2,1,0:T(1,128)} %reshape.12.routes_ref, bf16[128,2048]{1,0:T(8,128)(2,1)} %acts_ref.1, bf16[1024,768]{1,0:T(8,128)(2,1)} %bitcast.3, bf16[2048,768]{1,0:T(8,128)(2,1)} %bitcast.2, s32[16]{0:T(128)} %cluster_ref.1), custom_call_target="tpu_custom_call" | custom-call | flops 51539607552 | bytes 25165824 | tf_op jit(solution)/shard_map/pallas_call | solution.py:332
  204.8 3.8 %copy.10 = f32[8,128,768]{2,1,0:T(8,128)} copy(f32[8,128,768]{2,1,0:T(8,128)} %shard_map.55) | data formatting | bytes 6291456

commit v2 on v1

--- a/solution.py
+++ b/solution.py
@@ -8,8 +8,9 @@
 from jax.sharding import PartitionSpec as P
 
 PRIOR_WEIGHT = 1.0
-CHUNKS = 2
-X_LAG = 2
+CHUNKS = 4
+JOINED = 2
+X_LAG = 1
 VMEM_BYTES = 56 * 2**20
 GATHER_BYTES = 32 * 2**20
 
@@ -102,6 +103,7 @@
     nz = n // 4
     slab = act_v.shape[2]
     rows = g_v.shape[2]
+    span = rows * JOINED
     hidden = g_v.shape[3]
     fanout = rows * CHUNKS // act_v.shape[1]
     me = lax.axis_index("expert")
@@ -189,25 +191,25 @@
 
     acc[...] = jnp.zeros_like(acc)
     cnt[...] = jnp.zeros_like(cnt)
-    token = lax.broadcasted_iota(jnp.int32, (act_v.shape[1], rows), 0)
-    pair = lax.broadcasted_iota(jnp.int32, (act_v.shape[1], rows), 1)
-    for j in range(CHUNKS):
-        rep[j] = jnp.where(token == (pair + j * rows) // fanout, 1.0, 0.0).astype(jnp.bfloat16)
-
-    def add_block(b, j):
-        grad = g_v[b, j].astype(jnp.float32)
+    token = lax.broadcasted_iota(jnp.int32, (act_v.shape[1], span), 0)
+    pair = lax.broadcasted_iota(jnp.int32, (act_v.shape[1], span), 1)
+    for h in range(CHUNKS // JOINED):
+        rep[h] = jnp.where(token == (pair + h * span) // fanout, 1.0, 0.0).astype(jnp.bfloat16)
+
+    def add_block(b, h):
+        grad = g_v[b, pl.ds(h * JOINED, JOINED)].reshape(span, hidden).astype(jnp.float32)
         gsq[...] = (grad * grad).astype(jnp.bfloat16)
         act = act_v[b].astype(jnp.float32)
         sq_act = (act * act).astype(jnp.bfloat16)
         wide = lax.dot_general(
-            sq_act, rep[j], (((0,), (0,)), ((), ())), preferred_element_type=jnp.float32
+            sq_act, rep[h], (((0,), (0,)), ((), ())), preferred_element_type=jnp.float32
         ).astype(jnp.bfloat16)
-        named = rt_v[b, j]
-        ids = lax.broadcasted_iota(jnp.int32, (n, rows), 0)
+        named = rt_v[b, h]
+        ids = lax.broadcasted_iota(jnp.int32, (n, span), 0)
         mask = jnp.where(ids == named, 1.0, 0.0)
         cnt[...] += mask
         for e in range(n):
-            keep = jnp.broadcast_to(mask[e : e + 1].astype(jnp.bfloat16), (slab, rows))
+            keep = jnp.broadcast_to(mask[e : e + 1].astype(jnp.bfloat16), (slab, span))
             lhs[e * slab : (e + 1) * slab, :] = wide * keep
         step = 256 if hidden % 256 == 0 else hidden
         for k in range(0, hidden, step):
@@ -218,10 +220,61 @@
     turns = (nz + X_LAG) * CHUNKS
     burst = -(-(n - 1) // (turns // 2))
 
-    @pl.loop(0, turns)
+    def place(turn, q):
+        other_x = q // 2
+        up = lax.rem(q, 2)
+        j = lax.rem(turn, CHUNKS)
+        dist = turn // CHUNKS - X_LAG * other_x
+        z0 = z + (2 * up - 1) * dist
+        inside = (dist >= 0) & (dist < nz) & (z0 >= 0) & (z0 < nz)
+        column = z0 * 2 + lax.rem(x + other_x, 2)
+        return other_x, up, dist, j, column * 2, inside & ((dist > 0) | (up == 0))
+
+    def pass_on(turn, q):
+        other_x, up, dist, j, first, live = place(turn, q)
+        b = first + core
+
+        @pl.when(live)
+        def _():
+            arrived(g_v.at[b, j], g_recv.at[b, j])
+
+            @pl.when(b != me)
+            def _():
+                @pl.when((other_x == 0) & (up == 1) & (z > 0))
+                def _():
+                    g_copy(b, j, 0, me - 4).start()
+
+                @pl.when((other_x == 0) & (up == 0) & (z < nz - 1))
+                def _():
+                    g_copy(b, j, 1, me + 4).start()
+
+                @pl.when(other_x == 0)
+                def _():
+                    g_copy(b, j, 2, x_peer).start()
+
+                g_copy(b, j, 3, sibling).start()
+
+    def take(turn, q, other_core):
+        _, _, _, j, first, live = place(turn, q)
+        b = first + lax.rem(core + other_core, 2)
+
+        @pl.when(live)
+        def _():
+            @pl.when(other_core == 1)
+            def _():
+                arrived(g_v.at[b, j], g_recv.at[b, j])
+
+            @pl.when(j == 0)
+            def _():
+                arrived(rt_v.at[b], rt_recv.at[b])
+                arrived(act_v.at[b], act_recv.at[b])
+
+            @pl.when(lax.rem(j, JOINED) == JOINED - 1)
+            def _():
+                add_block(b, j // JOINED)
+
+    @pl.loop(0, turns + 1)
     def _(turn):
-        r = turn // CHUNKS
-        j = lax.rem(turn, CHUNKS)
         for k in range(burst):
             i = turn * burst + k + 1
 
@@ -229,42 +282,17 @@
             def _(i=i):
                 w_copy(far(i)).start()
 
-        @pl.loop(0, 8)
+        @pl.loop(0, 4)
         def _(q):
-            other_core = q // 4
-            other_x = lax.rem(q // 2, 2)
-            up = lax.rem(q, 2)
-            dist = r - X_LAG * other_x
-            z0 = z + (2 * up - 1) * dist
-            b = (z0 * 2 + lax.rem(x + other_x, 2)) * 2 + lax.rem(core + other_core, 2)
-            inside = (dist >= 0) & (dist < nz) & (z0 >= 0) & (z0 < nz)
-
-            @pl.when(inside & ((dist > 0) | (up == 0)))
-            def _():
-                arrived(g_v.at[b, j], g_recv.at[b, j])
-
-                @pl.when((other_core == 0) & (b != me))
-                def _():
-                    @pl.when(other_x == 0)
-                    def _():
-                        @pl.when((up == 1) & (z > 0))
-                        def _():
-                            g_copy(b, j, 0, me - 4).start()
-
-                        @pl.when((up == 0) & (z < nz - 1))
-                        def _():
-                            g_copy(b, j, 1, me + 4).start()
-
-                        g_copy(b, j, 2, x_peer).start()
-
-                    g_copy(b, j, 3, sibling).start()
-
-                @pl.when(j == 0)
-                def _():
-                    arrived(rt_v.at[b], rt_recv.at[b])
-                    arrived(act_v.at[b], act_recv.at[b])
-
-                add_block(b, j)
+            @pl.when(turn < turns)
+            def _():
+                pass_on(turn, q)
+
+            @pl.when(turn > 0)
+            def _():
+                @pl.loop(0, 2)
+                def _(other_core):
+                    take(turn - 1, q, other_core)
 
     share = 1.0 / jnp.sum(cnt[...], axis=1, keepdims=True)
     for e in range(n):
@@ -326,6 +354,7 @@
     slab = acts.shape[1] // n
     pairs = tok_rows * fanout
     rows = pairs // CHUNKS
+    span = rows * JOINED
     anywhere = pl.BlockSpec(memory_space=pl.ANY)
     dma = pltpu.SemaphoreType.DMA
     bf16 = jnp.bfloat16
@@ -335,15 +364,15 @@
         in_specs=[anywhere] * 4 + [pl.BlockSpec(memory_space=pltpu.SMEM)],
         out_specs=pl.BlockSpec(memory_space=pltpu.VMEM),
         scratch_shapes=[
-            pltpu.VMEM((n, CHUNKS, 1, rows), jnp.int32),
+            pltpu.VMEM((n, CHUNKS // JOINED, 1, span), jnp.int32),
             pltpu.VMEM((n, tok_rows, slab), bf16),
             pltpu.VMEM((n, CHUNKS, rows, hidden), bf16),
             pltpu.VMEM((n, slab, hidden), bf16),
             pltpu.VMEM((n, slab, hidden), jnp.float32),
-            pltpu.VMEM((n * slab, rows), bf16),
-            pltpu.VMEM((rows, hidden), bf16),
-            pltpu.VMEM((CHUNKS, tok_rows, rows), bf16),
-            pltpu.VMEM((n, rows), jnp.float32),
+            pltpu.VMEM((n * slab, span), bf16),
+            pltpu.VMEM((span, hidden), bf16),
+            pltpu.VMEM((CHUNKS // JOINED, tok_rows, span), bf16),
+            pltpu.VMEM((n, span), jnp.float32),
             pltpu.VMEM((n, 8, 128), jnp.float32),
             dma((n,)),
             dma((n,)),
@@ -363,7 +392,7 @@
             transcendentals=0,
         ),
     )(
-        routes.reshape(CHUNKS, 1, rows),
+        routes.reshape(CHUNKS // JOINED, 1, span),
         acts,
         grads.reshape(pairs, hidden),
         weights.reshape(n * slab, hidden),

time: 211 us -> 204 us (0.967); the launches traced: 209 us -> 204 us
  Pallas kernels: 203 us -> 199 us
    pallas_call x1, Pallas kernels: 203 us -> 199 us  [gathered(): pl.pallas_call(functools.partial(merge_kernel, n), out_shape=jax.ShapeDty...]
where the time goes in v2:
time: 204 us
  Pallas kernels  199 us (98%)
  local copies, waits for them, and re-layouts  5.27 us (3%)
    pallas_call x1, Pallas kernels, gathered(): pl.pallas_call(functools.partial(merge_kernel, n), out_shape=jax.ShapeDty...  199 us
    unnamed x2, local copies, waits for them, and re-layouts  4.57 us

profile of v2, /device:TPU:0, one launch (start us, length us, event | category | flops | bytes accessed | tf_op | source)
XLA Modules:
  0.0 204.1 jit_solution(824251247007873977)
XLA Ops:
  0.0 0.8 copy.7
  0.8 0.7 reshape.12.routes_ref
  1.5 198.8 %shard_map.55 = f32[8,128,768]{2,1,0:T(8,128)} custom-call(s32[2,1,512]{2,1,0:T(1,128)} %reshape.12.routes_ref, bf16[128,2048]{1,0:T(8,128)(2,1)} %acts_ref.1, bf16[1024,768]{1,0:T(8,128)(2,1)} %bitcast.3, bf16[2048,768]{1,0:T(8,128)(2,1)} %bitcast.2, s32[16]{0:T(128)} %cluster_ref.1), custom_call_target="tpu_custom_call" | custom-call | flops 51539607552 | bytes 25165824 | tf_op jit(solution)/shard_map/pallas_call | solution.py:361
  200.3 3.8 %copy.10 = f32[8,128,768]{2,1,0:T(8,128)} copy(f32[8,128,768]{2,1,0:T(8,128)} %shard_map.55) | data formatting | bytes 6291456

commit v3 on v2

--- a/solution.py
+++ b/solution.py
@@ -9,7 +9,7 @@
 
 PRIOR_WEIGHT = 1.0
 CHUNKS = 4
-JOINED = 2
+JOINED = 1
 X_LAG = 1
 VMEM_BYTES = 56 * 2**20
 GATHER_BYTES = 32 * 2**20

time: 204 us -> 207 us (1.015)
  Pallas kernels: 199 us -> 202 us
    pallas_call x1, Pallas kernels: 199 us -> 202 us  [gathered(): pl.pallas_call(functools.partial(merge_kernel, n), out_shape=jax.ShapeDty...]
where the time goes in v3:
time: 207 us
  Pallas kernels  202 us (98%)
  local copies, waits for them, and re-layouts  5.27 us (3%)
    pallas_call x1, Pallas kernels, gathered(): pl.pallas_call(functools.partial(merge_kernel, n), out_shape=jax.ShapeDty...  202 us
    unnamed x2, local copies, waits for them, and re-layouts  4.57 us

profile of v3, /device:TPU:0, one launch (start us, length us, event | category | flops | bytes accessed | tf_op | source)
XLA Modules:
  0.0 207.2 jit_solution(9085264434770575035)
XLA Ops:
  0.0 0.8 copy.7
  0.8 0.7 reshape.12.routes_ref
  1.5 201.9 %shard_map.55 = f32[8,128,768]{2,1,0:T(8,128)} custom-call(s32[4,1,256]{2,1,0:T(1,128)} %reshape.12.routes_ref, bf16[128,2048]{1,0:T(8,128)(2,1)} %acts_ref.1, bf16[1024,768]{1,0:T(8,128)(2,1)} %bitcast.3, bf16[2048,768]{1,0:T(8,128)(2,1)} %bitcast.2, s32[16]{0:T(128)} %cluster_ref.1), custom_call_target="tpu_custom_call" | custom-call | flops 51539607552 | bytes 25165824 | tf_op jit(solution)/shard_map/pallas_call | solution.py:361
  203.4 3.8 %copy.10 = f32[8,128,768]{2,1,0:T(8,128)} copy(f32[8,128,768]{2,1,0:T(8,128)} %shard_map.55) | data formatting | bytes 6291456
